TPU v7x, 32 devices: a whole 2x2x4 slice. The times are simulated.
32 devices in a mesh: expert: 16 (over z, y, x), ffn: 2 (over core).
Axes of the slice: x: 2, y: 2, z: 4, core: 2. Of those that a mesh axis runs over, the one named last changes fastest.
Arguments:
- tokens: bfloat16 [2048, 4096], P('expert'), may hold values from -6 to 6
- cotangent: bfloat16 [2048, 4096], P('expert'), may hold values from -6 to 6
- expert_ids: int32 [2048, 1], P('expert'), may hold values from 0 to 1; in each aligned block of 128 rows (0 to 127, 128 to 255, ...) at most 80 rows name the same one
- in_weight: bfloat16 [16, 512, 5120], P('expert', None, 'ffn'), may hold values from -0.09375 to 0.09375
- out_weight: bfloat16 [16, 5120, 512], P('expert', 'ffn'), may hold values from -0.078125 to 0.078125
- width_states: float32 [2, 2, 4096], replicated, may hold values from 76.8 to 768
- hidden_states: float32 [2, 2, 5120], P(None, None, 'ffn'), may hold values from 76.8 to 768
Outputs:
- update_in: bfloat16 [16, 512, 5120], P('expert', None, 'ffn')
- update_out: bfloat16 [16, 5120, 512], P('expert', 'ffn')
Inputs may be any that keep to these rules, and one draw needn't show every extreme that they name: `expert_ids`: within each block of 128 consecutive rows at most 80 name the same expert; in some block some expert is named by exactly 80 rows; every expert is named somewhere.
All inputs are finite; a program needn't handle non-finite values.
Results may differ from a plain program's by a relative error of at most 0.0049.
Values may be sent and summed in bfloat16 or wider, within the bound.
No kernel may reach another device: no remote copies, remote signals or barrier semaphores. Data moves between devices by JAX's collectives and lax.ppermute only.
A program may use at most 128 MiB of HBM per device.

v0:
```python
import math

import jax
import jax.numpy as jnp
from jax import lax
from jax.sharding import PartitionSpec as P

D = 4096
FF = 5120
GROUP = 8


DECAY_RATE = 0.9
EPS_ONE = 1e-30
ROOT_COEF = math.sqrt(2.0 / math.pi)
CUBIC_COEF = 0.044715


def partner_2(value, axis, bit):
    mask = 2**bit
    pairs = [(source, source ^ mask) for source in range(lax.axis_size(axis))]
    return lax.ppermute(value, axis, pairs)


def gelu_pair(inputs):
    inner = ROOT_COEF * (inputs + CUBIC_COEF * inputs * inputs * inputs)
    tangent = jnp.tanh(inner)
    act_value = 0.5 * inputs * (1.0 + tangent)
    act_slope = 0.5 * (1.0 + tangent) + 0.5 * inputs * (1.0 - tangent * tangent) * ROOT_COEF * (
        1.0 + 3.0 * CUBIC_COEF * inputs * inputs
    )
    return (act_value, act_slope)


def group_total(values):
    for section in range(GROUP.bit_length() - 1):
        values = values + partner_2(values, "expert", section)
    return values


def shards(tokens, cotangent, expert_ids, in_weight, out_weight, width_states, hidden_states):
    experts = width_states.shape[1]
    tok_rows = tokens.shape[0]
    capacity = 5 * tok_rows // (4 * experts)
    block_width = tokens.shape[1] // GROUP
    route_ids = expert_ids[:, 0]
    onehot = (route_ids[:, None] == jnp.arange(experts, dtype=jnp.int32)[None, :]).astype(jnp.int32)
    before = jnp.cumsum(onehot, axis=0) - onehot
    slot_index = jnp.sum(before * onehot, axis=1)
    target = slot_index * experts + route_ids
    select = (jnp.arange(capacity * experts, dtype=jnp.int32)[:, None] == target[None, :]).astype(
        jnp.bfloat16
    )
    sent_tokens = (
        jnp.dot(select, tokens, preferred_element_type=jnp.float32)
        .astype(jnp.bfloat16)
        .reshape(capacity, experts * GROUP, block_width)
    )
    sent_cotangent = (
        jnp.dot(select, cotangent, preferred_element_type=jnp.float32)
        .astype(jnp.bfloat16)
        .reshape(capacity, experts * GROUP, block_width)
    )
    got_tokens, got_cotangent = (
        lax.all_to_all(sent_tokens, "expert", split_axis=1, concat_axis=0, tiled=True),
        lax.all_to_all(sent_cotangent, "expert", split_axis=1, concat_axis=0, tiled=True),
    )
    expert_tokens = got_tokens.reshape(-1, block_width)
    expert_cotangent = got_cotangent.reshape(-1, block_width)
    local_in = in_weight[0]
    local_out = out_weight[0]
    pre_partial = jnp.dot(expert_tokens, local_in, preferred_element_type=jnp.float32)
    back_partial = lax.dot_general(
        expert_cotangent, local_out, (((1,), (1,)), ((), ())), preferred_element_type=jnp.float32
    )
    partials = jnp.stack([pre_partial, back_partial])
    position = lax.axis_index("expert")
    levels = GROUP.bit_length() - 1
    for section in range(levels):
        half_rows = partials.shape[1] // 2
        lower = partials[:, :half_rows]
        upper = partials[:, half_rows:]
        upper_side = position >> section & 1 == 1
        kept_rows = jnp.where(upper_side, upper, lower)
        sent_rows = jnp.where(upper_side, lower, upper)
        partials = kept_rows + partner_2(sent_rows, "expert", section)
    act_value, act_slope = gelu_pair(partials[0])
    shares = jnp.stack(
        [act_value.astype(jnp.bfloat16), (partials[1] * act_slope).astype(jnp.bfloat16)]
    )
    for section in reversed(range(levels)):
        partner = partner_2(shares, "expert", section)
        upper_side = position >> section & 1 == 1
        shares = jnp.where(
            upper_side,
            jnp.concatenate([partner, shares], axis=1),
            jnp.concatenate([shares, partner], axis=1),
        )
    hidden = shares[0]
    pre_grad = shares[1]
    grad_in = lax.dot_general(
        expert_tokens, pre_grad, (((0,), (0,)), ((), ())), preferred_element_type=jnp.float32
    )
    grad_out = lax.dot_general(
        hidden, expert_cotangent, (((0,), (0,)), ((), ())), preferred_element_type=jnp.float32
    )
    expert = position // GROUP
    block_index = position % GROUP
    width_pick = lax.dynamic_index_in_dim(width_states, expert, 1, keepdims=False)
    width_local = lax.dynamic_slice_in_dim(width_pick, block_index * block_width, block_width, 1)
    hidden_local = lax.dynamic_index_in_dim(hidden_states, expert, 1, keepdims=False)
    square_in = grad_in * grad_in + EPS_ONE
    square_out = grad_out * grad_out + EPS_ONE
    pair_sums = group_total(jnp.stack([jnp.sum(square_in, axis=0), jnp.sum(square_out, axis=1)]))
    small_totals = jnp.stack(
        [jnp.sum(pair_sums[0]), jnp.sum(pair_sums[1]), jnp.sum(hidden_local[1])]
    )
    row_in, col_out, totals = lax.psum(
        (jnp.sum(square_in, axis=1), jnp.sum(square_out, axis=0), small_totals), "ffn"
    )
    whole_count = float(D) * float(FF)
    rows_in = DECAY_RATE * width_local[0] + (1.0 - DECAY_RATE) * row_in / FF
    cols_in = DECAY_RATE * hidden_local[0] + (1.0 - DECAY_RATE) * pair_sums[0] / D
    mean_in = DECAY_RATE * jnp.mean(width_pick[0]) + (1.0 - DECAY_RATE) * totals[0] / whole_count
    rows_out = DECAY_RATE * hidden_local[1] + (1.0 - DECAY_RATE) * pair_sums[1] / D
    cols_out = DECAY_RATE * width_local[1] + (1.0 - DECAY_RATE) * col_out / FF
    mean_out = DECAY_RATE * totals[2] / FF + (1.0 - DECAY_RATE) * totals[1] / whole_count
    raw_in = grad_in * lax.rsqrt(rows_in[:, None] * cols_in[None, :] / mean_in)
    raw_out = grad_out * lax.rsqrt(rows_out[:, None] * cols_out[None, :] / mean_out)
    norm_sums = group_total(jnp.stack([jnp.sum(raw_in * raw_in), jnp.sum(raw_out * raw_out)]))
    norm_sums = lax.psum(norm_sums, "ffn")
    clip_ratio = jnp.sqrt(norm_sums / whole_count)
    update_in = (raw_in / jnp.maximum(1.0, clip_ratio[0])).astype(jnp.bfloat16)[None]
    update_out = (raw_out / jnp.maximum(1.0, clip_ratio[1])).astype(jnp.bfloat16)[None]
    return (update_in, update_out)


def solution(mesh):
    return jax.shard_map(
        shards,
        mesh=mesh,
        in_specs=(
            P("expert", None),
            P("expert", None),
            P("expert", None),
            P("expert", None, "ffn"),
            P("expert", "ffn", None),
            P(),
            P(None, None, "ffn"),
        ),
        out_specs=(P("expert", None, "ffn"), P("expert", "ffn", None)),
        check_vma=False,
    )
```

profile of v0, /device:TPU:1, one launch (start us, length us, event | category | flops | bytes accessed | tf_op | source)
XLA Modules:
  0.0 955.1 jit_solution(3758167070909238548)
XLA Ops:
  3.2 2.8 convolution_convert_fusion
  6.0 3.3 reshape.83
  9.3 3.1 copy.12
  12.3 7.5 all-to-all-start.1
  19.8 2.8 convolution_convert_fusion.1
  22.6 3.3 reshape.81
  25.9 3.1 copy.11
  29.0 18.0 %all-to-all-done.1 = bf16[80,16,512]{2,0,1:T(8,128)(2,1)} async-done(((bf16[80,16,512]{2,0,1:T(8,128)(2,1)}), bf16[80,16,512]{2,0,1:T(8,128)(2,1)}, u32[]{:S(2)}, u32[]{:S(2)}) %all-to-all-start.1) | async-done | bytes 1310752 | tf_op jit(solution)/shard_map/all_to_all | solution.py:66
  46.9 8.0 all-to-all-start
  54.9 8.1 convolution_bitcast_fusion
  63.0 19.0 %all-to-all-done = bf16[80,16,512]{2,0,1:T(8,128)(2,1)} async-done(((bf16[80,16,512]{2,0,1:T(8,128)(2,1)}), bf16[80,16,512]{2,0,1:T(8,128)(2,1)}, u32[]{:S(2)}, u32[]{:S(2)}) %all-to-all-start) | async-done | bytes 1310752 | tf_op jit(solution)/shard_map/all_to_all | solution.py:65
  82.0 5.9 convolution_bitcast_fusion.1
  87.9 7.3 broadcast_select_fusion
  95.2 1.4 copy-done.5
  96.6 280.0 %collective-permute-done = f32[2,640,2560]{2,1,0:T(8,128)} collective-permute-done((f32[2,640,2560]{2,1,0:T(8,128)}, f32[2,640,2560]{2,1,0:T(8,128)}, u32[]{:S(2)}, u32[]{:S(2)}) %collective-permute-start) | collective-permute-done | bytes 13107232 | tf_op jit(solution)/shard_map/ppermute | solution.py:22
  376.6 13.8 %select_add_fusion = f32[2,640,2560]{2,1,0:T(8,128)S(1)} fusion(f32[2,640,2560]{2,1,0:T(8,128)} %collective-permute-done, pred[]{:T(512)S(6)} %eq.49, f32[1,1280,2560]{2,1,0:T(8,128)} %convolution_bitcast_fusion, f32[1,1280,2560]{2,1,0:T(8,128)} %copy-done.5), kind=kLoop, calls=%fused_computation.5 | loop fusion | flops 13107200 | bytes 52428800 | tf_op jit(solution)/shard_map/add | solution.py:86
  390.4 4.7 slice_select_fusion
  395.1 2.1 copy-done.2
  397.2 3.8 collective-permute-start.1
  401.0 138.3 %collective-permute-done.1 = f32[2,320,2560]{2,1,0:T(8,128)} collective-permute-done((f32[2,320,2560]{2,1,0:T(8,128)}, f32[2,320,2560]{2,1,0:T(8,128)}, u32[]{:S(2)}, u32[]{:S(2)}) %collective-permute-start.1) | collective-permute-done | bytes 6553632 | tf_op jit(solution)/shard_map/ppermute | solution.py:22
  539.3 11.5 %select_add_fusion.1 = f32[2,320,2560]{2,1,0:T(8,128)} fusion(f32[2,320,2560]{2,1,0:T(8,128)} %collective-permute-done.1, f32[2,640,2560]{2,1,0:T(8,128)} %copy-done.2, pred[]{:T(512)S(6)} %eq.50), kind=kLoop, calls=%fused_computation.13 | loop fusion | flops 3276800 | bytes 26214400 | tf_op jit(solution)/shard_map/add | solution.py:86
  550.8 3.5 slice_select_fusion.1
  554.3 6.0 collective-permute-start.2
  560.3 68.2 %collective-permute-done.2 = f32[2,160,2560]{2,1,0:T(8,128)S(1)} collective-permute-done((f32[2,160,2560]{2,1,0:T(8,128)S(1)}, f32[2,160,2560]{2,1,0:T(8,128)S(1)}, u32[]{:S(2)}, u32[]{:S(2)}) %collective-permute-start.2) | collective-permute-done | bytes 3276832 | tf_op jit(solution)/shard_map/ppermute | solution.py:22
  630.7 1.2 collective-permute-start.3
  631.9 32.4 %collective-permute-done.3 = bf16[2,160,2560]{2,1,0:T(8,128)(2,1)S(1)} collective-permute-done((bf16[2,160,2560]{2,1,0:T(8,128)(2,1)S(1)}, bf16[2,160,2560]{2,1,0:T(8,128)(2,1)S(1)}, u32[]{:S(2)}, u32[]{:S(2)}) %collective-permute-start.3) | collective-permute-done | bytes 1638432 | tf_op jit(solution)/shard_map/ppermute | solution.py:22
  666.0 67.2 %collective-permute-done.4 = bf16[2,320,2560]{2,1,0:T(8,128)(2,1)S(1)} collective-permute-done((bf16[2,320,2560]{2,1,0:T(8,128)(2,1)S(1)}, bf16[2,320,2560]{2,1,0:T(8,128)(2,1)S(1)}, u32[]{:S(2)}, u32[]{:S(2)}) %collective-permute-start.4) | collective-permute-done | bytes 3276832 | tf_op jit(solution)/shard_map/ppermute | solution.py:22
  733.1 1.8 maximum_select_fusion.1
  735.1 137.0 %collective-permute-done.5 = bf16[2,640,2560]{2,1,0:T(8,128)(2,1)S(1)} collective-permute-done((bf16[2,640,2560]{2,1,0:T(8,128)(2,1)S(1)}, bf16[2,640,2560]{2,1,0:T(8,128)(2,1)S(1)}, u32[]{:S(2)}, u32[]{:S(2)}) %collective-permute-start.5) | collective-permute-done | bytes 6553632 | tf_op jit(solution)/shard_map/ppermute | solution.py:22
  872.1 7.2 maximum_select_fusion
  879.3 7.1 fusion.4
  886.4 7.0 fusion.5
  893.6 2.6 collective-permute-done.6
  896.3 2.6 collective-permute-done.7
  900.1 1.4 dynamic-slice_reduce_fusion
  903.5 2.0 pad_maximum_fusion.3
  905.6 11.4 %all-reduce = (f32[3]{0:T(128)S(1)}, f32[512]{0:T(512)S(1)}, f32[512]{0:T(512)S(1)}) all-reduce(f32[3]{0:T(128)S(1)} %pad_maximum_fusion.3, f32[512]{0:T(512)S(1)} %get-tuple-element.4, f32[512]{0:T(512)S(1)} %get-tuple-element.2), channel_id=1, replica_groups=mesh['expert'=16,'ffn'=2] {'ffn'}, use_global_device_ids=true, to_apply=%region_10.11 | all-reduce | flops 1027 | bytes 8216 | tf_op jit(solution)/shard_map/psum | solution.py:118
  919.8 4.8 multiply_reduce_fusion.1
  924.6 2.9 multiply_reduce_fusion
  927.4 1.4 pad_maximum_fusion.4
  928.9 2.3 collective-permute-done.9
  931.2 1.4 fusion.33
  932.9 2.0 collective-permute-done.10
  935.0 1.4 fusion.35
  937.2 1.5 collective-permute-done.11
  938.8 5.9 psum.31
  945.9 4.4 fusion.10
  951.0 4.1 fusion.9
  (47 shorter events, 11.9 us)
Async XLA Ops:
  0.6 54.3 %copy-start = (bf16[1,2560,512]{2,1,0:T(8,128)(2,1)S(1)}, bf16[1,2560,512]{2,1,0:T(8,128)(2,1)}, u32[]{:S(2)}) copy-start(bf16[1,2560,512]{2,1,0:T(8,128)(2,1)} %param.11) | copy-start | bytes 7864324
  12.3 34.6 %all-to-all-start.1 = ((bf16[80,16,512]{2,0,1:T(8,128)(2,1)}), bf16[80,16,512]{2,0,1:T(8,128)(2,1)}, u32[]{:S(2)}, u32[]{:S(2)}) async-start(bf16[80,16,512]{2,0,1:T(8,128)(2,1)} %copy.12), calls=%async_computation.1 | async-start | bytes 2621440 | tf_op jit(solution)/shard_map/all_to_all | solution.py:66
  46.9 35.1 %all-to-all-start = ((bf16[80,16,512]{2,0,1:T(8,128)(2,1)}), bf16[80,16,512]{2,0,1:T(8,128)(2,1)}, u32[]{:S(2)}, u32[]{:S(2)}) async-start(bf16[80,16,512]{2,0,1:T(8,128)(2,1)} %copy.11), calls=%async_computation | async-start | bytes 2621440 | tf_op jit(solution)/shard_map/all_to_all | solution.py:65
  82.0 5.9 copy-start.4
  87.9 8.7 copy-start.5
  96.6 280.0 %collective-permute-start = (f32[2,640,2560]{2,1,0:T(8,128)}, f32[2,640,2560]{2,1,0:T(8,128)}, u32[]{:S(2)}, u32[]{:S(2)}) collective-permute-start(f32[2,640,2560]{2,1,0:T(8,128)} %broadcast_select_fusion), channel_id=1, source_target_pairs={{0,2},{2,0},{4,6},{6,4},{8,10},{10,8},{12,14},{14,12},{16,18},{18,... | collective-permute-start | bytes 39321608 | tf_op jit(solution)/shard_map/ppermute | solution.py:22
  390.4 6.8 copy-start.2
  397.2 142.1 %collective-permute-start.1 = (f32[2,320,2560]{2,1,0:T(8,128)}, f32[2,320,2560]{2,1,0:T(8,128)}, u32[]{:S(2)}, u32[]{:S(2)}) collective-permute-start(f32[2,320,2560]{2,1,0:T(8,128)} %slice_select_fusion), channel_id=1, source_target_pairs={{0,4},{2,6},{4,0},{6,2},{8,12},{10,14},{12,8},{14,10},{16,20},{18,... | collective-permute-start | bytes 19660808 | tf_op jit(solution)/shard_map/ppermute | solution.py:22
  550.8 77.7 %copy-start.3 = (f32[2,320,2560]{2,1,0:T(8,128)S(1)}, f32[2,320,2560]{2,1,0:T(8,128)}, u32[]{:S(2)}) copy-start(f32[2,320,2560]{2,1,0:T(8,128)} %select_add_fusion.1) | copy-start | bytes 19660804
  554.3 74.2 %collective-permute-start.2 = (f32[2,160,2560]{2,1,0:T(8,128)S(1)}, f32[2,160,2560]{2,1,0:T(8,128)S(1)}, u32[]{:S(2)}, u32[]{:S(2)}) collective-permute-start(f32[2,160,2560]{2,1,0:T(8,128)S(1)} %slice_select_fusion.1), channel_id=1, source_target_pairs={{0,8},{2,10},{4,12},{6,14},{8,0},{10,2},{12,4},{14,6},{16,24},{18,... | collective-permute-start | bytes 9830408 | tf_op jit(solution)/shard_map/ppermute | solution.py:22
  630.7 33.7 %collective-permute-start.3 = (bf16[2,160,2560]{2,1,0:T(8,128)(2,1)S(1)}, bf16[2,160,2560]{2,1,0:T(8,128)(2,1)S(1)}, u32[]{:S(2)}, u32[]{:S(2)}) collective-permute-start(bf16[2,160,2560]{2,1,0:T(8,128)(2,1)S(1)} %pad_maximum_fusion.1), channel_id=1, source_target_pairs={{0,8},{2,10},{4,12},{6,14},{8,0},{10,2},{12,4},{14,6},{16,24},{18,... | collective-permute-start | bytes 4915208 | tf_op jit(solution)/shard_map/ppermute | solution.py:22
  665.3 67.9 %collective-permute-start.4 = (bf16[2,320,2560]{2,1,0:T(8,128)(2,1)S(1)}, bf16[2,320,2560]{2,1,0:T(8,128)(2,1)S(1)}, u32[]{:S(2)}, u32[]{:S(2)}) collective-permute-start(bf16[2,320,2560]{2,1,0:T(8,128)(2,1)S(1)} %maximum_select_fusion.2), channel_id=1, source_target_pairs={{0,4},{2,6},{4,0},{6,2},{8,12},{10,14},{12,8},{14,10},{16,20},{18,... | collective-permute-start | bytes 9830408 | tf_op jit(solution)/shard_map/ppermute | solution.py:22
  734.9 137.2 %collective-permute-start.5 = (bf16[2,640,2560]{2,1,0:T(8,128)(2,1)S(1)}, bf16[2,640,2560]{2,1,0:T(8,128)(2,1)S(1)}, u32[]{:S(2)}, u32[]{:S(2)}) collective-permute-start(bf16[2,640,2560]{2,1,0:T(8,128)(2,1)S(1)} %maximum_select_fusion.1), channel_id=1, source_target_pairs={{0,2},{2,0},{4,6},{6,4},{8,10},{10,8},{12,14},{14,12},{16,18},{18,... | collective-permute-start | bytes 19660808 | tf_op jit(solution)/shard_map/ppermute | solution.py:22
  886.4 15.8 %copy-start.7 = (f32[2,2,2560]{2,1,0:T(2,128)S(1)}, f32[2,2,2560]{2,1,0:T(2,128)}, u32[]{:S(2)}) copy-start(f32[2,2,2560]{2,1,0:T(2,128)} %param.13) | copy-start | bytes 122884
  893.5 2.7 collective-permute-start.6
  896.2 2.7 collective-permute-start.7
  898.9 3.9 collective-permute-start.8
  918.9 5.6 copy-start.6
  928.8 2.4 collective-permute-start.9
  932.6 2.4 collective-permute-start.10
  936.4 2.4 collective-permute-start.11
  945.9 9.2 copy-start.1
where the time goes:
time: 956 us; the launch traced here: 955 us
  waiting for transfers between devices  771 us (81%)
  other arithmetic  81.4 us (9%)
  matrix products  33.6 us (4%)
  starting transfers between devices  29.2 us (3%)
  local copies, waits for them, and re-layouts  17.5 us (2%)
  blocking collectives  17.3 us (2%)
    ppermute x12, waiting for transfers between devices, partner_2(): return lax.ppermute(value, axis, pairs)  734 us
    add x3, other arithmetic, shards(): partials = kept_rows + partner_2(sent_rows, 'expert', section)  26.2 us
  transfers between devices with their start and end apart: 14, of which 13 were waited for; matrix products, arithmetic and copies ran while one was open for 2% of the time, Pallas kernels for 0%

commit v1 on v0

v1 whole, which is shorter than its diff:
```python
import math

import jax
import jax.numpy as jnp
from jax import lax
from jax.sharding import PartitionSpec as P

D = 4096
FF = 5120
GROUP = 8


DECAY_RATE = 0.9
EPS_ONE = 1e-30
ROOT_COEF = math.sqrt(2.0 / math.pi)
CUBIC_COEF = 0.044715

PAIR, FIRST, SECOND = 1, 2, 4


def swap(value, mask, axis="expert"):
    pairs = [(source, source ^ mask) for source in range(lax.axis_size(axis))]
    return lax.ppermute(value, axis, pairs)


def gelu_pair(inputs):
    inner = ROOT_COEF * (inputs + CUBIC_COEF * inputs * inputs * inputs)
    tangent = jnp.tanh(inner)
    act_value = 0.5 * inputs * (1.0 + tangent)
    act_slope = 0.5 * (1.0 + tangent) + 0.5 * inputs * (1.0 - tangent * tangent) * ROOT_COEF * (
        1.0 + 3.0 * CUBIC_COEF * inputs * inputs
    )
    return (act_value, act_slope)


def dot(left, right, left_dim, right_dim):
    return lax.dot_general(
        left, right, (((left_dim,), (right_dim,)), ((), ())), preferred_element_type=jnp.float32
    )


def scalar_total(values):
    first = values
    for mask in (FIRST, SECOND, FIRST | SECOND):
        first = first + swap(values, mask)
    second = first + swap(first, PAIR)
    return lax.psum(second, "ffn")


def shards(tokens, cotangent, expert_ids, in_weight, out_weight, width_states, hidden_states):
    bf16 = jnp.bfloat16
    experts = width_states.shape[1]
    tok_rows, width = tokens.shape
    capacity = 5 * tok_rows // (4 * experts)
    part_cap = capacity // 2
    places = lax.axis_size("expert")
    block_width = width // GROUP
    hidden_part = in_weight.shape[2] // 2
    position = lax.axis_index("expert")
    expert = position // GROUP
    block_index = position % GROUP
    part = lax.axis_index("ffn") % 2
    pair_bit = position & 1
    first_bit = position >> 1 & 1
    second_bit = position >> 2 & 1

    local_in = in_weight[0]
    local_out = out_weight[0]
    keep_at = pair_bit * hidden_part
    send_at = (1 - pair_bit) * hidden_part
    in_keep = lax.dynamic_slice_in_dim(local_in, keep_at, hidden_part, 1)
    in_got = swap(lax.dynamic_slice_in_dim(local_in, send_at, hidden_part, 1), PAIR)
    out_keep = lax.dynamic_slice_in_dim(local_out, keep_at, hidden_part, 0)
    out_got = swap(lax.dynamic_slice_in_dim(local_out, send_at, hidden_part, 0), PAIR)

    route_ids = expert_ids[:, 0]
    onehot = (route_ids[:, None] == jnp.arange(experts, dtype=jnp.int32)[None, :]).astype(jnp.int32)
    before = jnp.cumsum(onehot, axis=0) - onehot
    slot_index = jnp.sum(before * onehot, axis=1) - part * part_cap
    valid = (slot_index >= 0) & (slot_index < part_cap)
    target = jnp.where(valid, route_ids * part_cap + slot_index, -1)
    select = (jnp.arange(experts * part_cap, dtype=jnp.int32)[:, None] == target[None, :]).astype(bf16)

    def dispatch(values):
        routed = dot(select, values, 1, 0).astype(bf16)
        routed = routed.reshape(experts, part_cap, GROUP, block_width).transpose(0, 2, 1, 3)
        routed = routed.reshape(places, part_cap, block_width)
        got = lax.all_to_all(routed, "expert", split_axis=0, concat_axis=0, tiled=True)
        got = got.reshape(places // GROUP, 2, 2, 2 * part_cap, block_width)
        got = jnp.where(second_bit == 1, got[:, ::-1], got)
        got = jnp.where(first_bit == 1, got[:, :, ::-1], got)
        got = got.transpose(1, 2, 0, 3, 4).reshape(4, -1, block_width)
        wide = jnp.concatenate([got, swap(got, PAIR)], axis=2)
        rows = jnp.concatenate([wide, swap(wide, 1, "ffn")], axis=1)
        return rows.reshape(2, 2, -1, 2 * block_width)

    expert_tokens = dispatch(tokens)
    expert_cotangent = dispatch(cotangent)
    in_pair = jnp.concatenate([in_keep, in_got], axis=0)
    out_pair = jnp.concatenate([out_keep, out_got], axis=1)

    middle = (hidden_part // 128 + 1) // 2 * 128 if hidden_part >= 256 else hidden_part // 2
    bounds = ((0, middle), (middle, hidden_part))
    orders = ((FIRST, SECOND, 1), (SECOND, FIRST, 0))

    def scatter_sum(rows, weights, contract, order):
        mask_one, mask_two, dim = order
        kept_rows = lax.index_in_dim(rows, 0, dim, keepdims=False)
        sent_rows = lax.index_in_dim(rows, 1, dim, keepdims=False)
        got = swap(dot(sent_rows, weights, 2, contract).astype(bf16), mask_one)
        total = dot(kept_rows, weights, 2, contract) + got.astype(jnp.float32)
        got = swap(total[1].astype(bf16), mask_two)
        return total[0] + got.astype(jnp.float32)

    def gather(own, order):
        mask_one, mask_two, dim = order
        both = jnp.stack([own, swap(own, mask_two)])
        whole = jnp.stack([both, swap(both, mask_one)], axis=dim)
        return whole.reshape(-1, own.shape[-1])

    pre = [
        scatter_sum(expert_tokens, in_pair[:, low:high], 0, order)
        for (low, high), order in zip(bounds, orders)
    ]
    back = [
        scatter_sum(expert_cotangent, out_pair[low:high], 1, order)
        for (low, high), order in zip(bounds, orders)
    ]
    acts = [gelu_pair(value) for value in pre]
    hidden = [gather(act[0].astype(bf16), order) for act, order in zip(acts, orders)]
    pre_grad = [
        gather((value * act[1]).astype(bf16), order) for value, act, order in zip(back, acts, orders)
    ]
    token_rows = expert_tokens.reshape(-1, 2 * block_width)
    cotangent_rows = expert_cotangent.reshape(-1, 2 * block_width)

    width_pick = lax.dynamic_index_in_dim(width_states, expert, 1, keepdims=False)
    width_pair = jnp.concatenate(
        [
            lax.dynamic_slice_in_dim(width_pick, block_index * block_width, block_width, 1),
            lax.dynamic_slice_in_dim(width_pick, (block_index ^ 1) * block_width, block_width, 1),
        ],
        axis=1,
    )
    hidden_pick = lax.dynamic_index_in_dim(hidden_states, expert, 1, keepdims=False)
    hidden_own = lax.dynamic_slice_in_dim(hidden_pick, keep_at, hidden_part, 1)
    hidden_mean = lax.psum(jnp.sum(hidden_pick[1]), "ffn") / FF
    width_mean = jnp.mean(width_pick[0])

    def sums_width(partial):
        got = swap(partial, PAIR)
        total = partial + jnp.concatenate([got[block_width:], got[:block_width]])
        return lax.psum(total, "ffn")

    def sums_hidden(partial):
        total = partial
        for mask in (FIRST, SECOND, FIRST | SECOND):
            total = total + swap(partial, mask)
        return total

    whole_count = float(D) * float(FF)

    grad_out = jnp.concatenate([dot(value, cotangent_rows, 0, 0) for value in hidden], axis=0)
    out_received = swap(grad_out[:, block_width:].astype(bf16), PAIR)
    square_out = grad_out * grad_out + EPS_ONE
    row_out = jnp.sum(square_out, axis=1)
    col_out = jnp.sum(square_out, axis=0)
    rows_out = DECAY_RATE * hidden_own[1] + (1.0 - DECAY_RATE) * sums_hidden(row_out) / D
    cols_out = DECAY_RATE * width_pair[1] + (1.0 - DECAY_RATE) * sums_width(col_out) / FF
    norm_out = jnp.sum(square_out_scaled(grad_out, rows_out, cols_out))
    total_out, norm_out = scalar_total(jnp.stack([jnp.sum(row_out), norm_out]))
    mean_out = DECAY_RATE * hidden_mean + (1.0 - DECAY_RATE) * total_out / whole_count
    clip_out = jnp.maximum(1.0, jnp.sqrt(mean_out * norm_out / whole_count))
    factor_out = jnp.sqrt(mean_out) / clip_out
    rows_out_got = swap(rows_out, PAIR)

    grad_in = jnp.concatenate([dot(token_rows, value, 0, 0) for value in pre_grad], axis=1)
    in_received = swap(grad_in[block_width:].astype(bf16), PAIR)
    square_in = grad_in * grad_in + EPS_ONE
    row_in = jnp.sum(square_in, axis=1)
    col_in = jnp.sum(square_in, axis=0)
    rows_in = DECAY_RATE * width_pair[0] + (1.0 - DECAY_RATE) * sums_width(row_in) / FF
    cols_in = DECAY_RATE * hidden_own[0] + (1.0 - DECAY_RATE) * sums_hidden(col_in) / D
    norm_in = jnp.sum(square_out_scaled(grad_in, rows_in, cols_in))
    total_in, norm_in = scalar_total(jnp.stack([jnp.sum(row_in), norm_in]))
    mean_in = DECAY_RATE * width_mean + (1.0 - DECAY_RATE) * total_in / whole_count
    clip_in = jnp.maximum(1.0, jnp.sqrt(mean_in * norm_in / whole_count))
    factor_in = jnp.sqrt(mean_in) / clip_in
    cols_in_got = swap(cols_in, PAIR)

    def finish(grad, rows, cols, factor):
        scale = lax.rsqrt(rows)[:, None] * lax.rsqrt(cols)[None, :] * factor
        return (grad.astype(jnp.float32) * scale).astype(bf16)

    in_own = finish(grad_in[:block_width], rows_in[:block_width], cols_in, factor_in)
    in_other = finish(in_received, rows_in[:block_width], cols_in_got, factor_in)
    update_in = jnp.where(
        pair_bit == 1,
        jnp.concatenate([in_other, in_own], axis=1),
        jnp.concatenate([in_own, in_other], axis=1),
    )
    out_own = finish(grad_out[:, :block_width], rows_out, cols_out[:block_width], factor_out)
    out_other = finish(out_received, rows_out_got, cols_out[:block_width], factor_out)
    update_out = jnp.where(
        pair_bit == 1,
        jnp.concatenate([out_other, out_own], axis=0),
        jnp.concatenate([out_own, out_other], axis=0),
    )
    return (update_in[None], update_out[None])


def square_out_scaled(grad, rows, cols):
    return grad * grad * (1.0 / rows)[:, None] * (1.0 / cols)[None, :]


def solution(mesh):
    return jax.shard_map(
        shards,
        mesh=mesh,
        in_specs=(
            P("expert", None),
            P("expert", None),
            P("expert", None),
            P("expert", None, "ffn"),
            P("expert", "ffn", None),
            P(),
            P(None, None, "ffn"),
        ),
        out_specs=(P("expert", None, "ffn"), P("expert", "ffn", None)),
        check_vma=False,
    )
```

time: 956 us -> 335 us (0.35)
  waiting for transfers between devices: 771 us -> 165 us
  starting transfers between devices: 29.2 us -> 76.8 us
  other arithmetic: 81.4 us -> 41.5 us
  matrix products: 33.6 us -> 18.1 us
    ppermute x12 -> x42, waiting for transfers between devices: 734 us -> 139 us  [swap(): return lax.ppermute(value, axis, pairs)]
    ppermute x12 -> x42, starting transfers between devices: 13.8 us -> 62.7 us  [swap(): return lax.ppermute(value, axis, pairs)]
    add x13 -> x6, other arithmetic: 30.4 us -> 2.54 us  [the longest x2 2.51 us: scalar_total(): first = first + swap(values, mask)]
    select_n x6 -> x4, other arithmetic: 25.4 us -> 4.74 us  [the longest x1 1.92 us: shards(): jnp.where(pair_bit == 1, jnp.concatenate([in_other, in_own], axis=1), jnp...]
    dot_general x6 -> x14, matrix products: 33.6 us -> 18.1 us  [dot(): lax.dot_general(left, right, (((left_dim,), (right_dim,)), ((), ())), pre...]
    reshape x4 -> x2, local copies, waits for them, and re-layouts: 12.7 us -> 2.06 us  [dispatch(): routed.reshape(experts, part_cap, GROUP, block_width).transpose(0, 2, 1, 3)]
    all_to_all x2, waiting for transfers between devices: 37 us -> 26.4 us  [dispatch(): lax.all_to_all(routed, 'expert', split_axis=0, concat_axis=0, tiled=True)]
  transfers between devices with their start and end apart: 14 -> 44, of which waited for: 13 -> 16; matrix products, arithmetic and copies ran while one was open for 2% -> 19% of each run, Pallas kernels for 0% -> 0%
where the time goes in v1:
time: 335 us; the launch traced here: 334 us
  waiting for transfers between devices  165 us (49%)
  starting transfers between devices  76.8 us (23%)
  other arithmetic  41.5 us (12%)
  matrix products  18.1 us (5%)
  local copies, waits for them, and re-layouts  14.8 us (4%)
  blocking collectives  12.1 us (4%)
  between operations  5.16 us (2%)
    ppermute x42, waiting for transfers between devices, swap(): return lax.ppermute(value, axis, pairs)  139 us
    ppermute x42, starting transfers between devices, swap(): return lax.ppermute(value, axis, pairs)  62.7 us
    all_to_all x2, waiting for transfers between devices, dispatch(): lax.all_to_all(routed, 'expert', split_axis=0, concat_axis=0, tiled=True)  26.4 us
    dot_general x14, matrix products, dot(): lax.dot_general(left, right, (((left_dim,), (right_dim,)), ((), ())), pre...  18.1 us
    all_to_all x2, starting transfers between devices, dispatch(): lax.all_to_all(routed, 'expert', split_axis=0, concat_axis=0, tiled=True)  14.1 us
    unnamed x40, local copies, waits for them, and re-layouts  8.09 us
    psum x1, blocking collectives, sums_width(): return lax.psum(total, 'ffn')  7.61 us
  transfers between devices with their start and end apart: 44, of which 16 were waited for; matrix products, arithmetic and copies ran while one was open for 19% of the time, Pallas kernels for 0%

profile of v1, /device:TPU:1, one launch (start us, length us, event | category | flops | bytes accessed | tf_op | source)
XLA Modules:
  0.0 334.0 jit_solution(15462128512198863775)
XLA Ops:
  4.8 7.4 %all-to-all-start.1 = ((bf16[16,40,512]{2,1,0:T(8,128)(2,1)}), bf16[16,40,512]{2,1,0:T(8,128)(2,1)S(1)}, u32[]{:S(2)}, u32[]{:S(2)}) async-start(bf16[16,40,512]{2,1,0:T(8,128)(2,1)} %bitcast.8), calls=%async_computation.1 | async-start | bytes 1310720 | tf_op jit(solution)/shard_map/all_to_all | solution.py:88
  13.8 12.8 %all-to-all-done.1 = bf16[16,40,512]{2,1,0:T(8,128)(2,1)S(1)} async-done(((bf16[16,40,512]{2,1,0:T(8,128)(2,1)}), bf16[16,40,512]{2,1,0:T(8,128)(2,1)S(1)}, u32[]{:S(2)}, u32[]{:S(2)}) %all-to-all-start.1) | async-done | bytes 655392 | tf_op jit(solution)/shard_map/all_to_all | solution.py:88
  26.6 6.7 %all-to-all-start = ((bf16[16,40,512]{2,1,0:T(8,128)(2,1)}), bf16[16,40,512]{2,1,0:T(8,128)(2,1)S(1)}, u32[]{:S(2)}, u32[]{:S(2)}) async-start(bf16[16,40,512]{2,1,0:T(8,128)(2,1)} %bitcast.2), calls=%async_computation | async-start | bytes 1310720 | tf_op jit(solution)/shard_map/all_to_all | solution.py:88
  33.3 13.6 %all-to-all-done = bf16[16,40,512]{2,1,0:T(8,128)(2,1)S(1)} async-done(((bf16[16,40,512]{2,1,0:T(8,128)(2,1)}), bf16[16,40,512]{2,1,0:T(8,128)(2,1)S(1)}, u32[]{:S(2)}, u32[]{:S(2)}) %all-to-all-start) | async-done | bytes 655392 | tf_op jit(solution)/shard_map/all_to_all | solution.py:88
  48.3 1.9 dynamic-slice_bitcast_fusion.1
  52.0 7.9 %collective-permute-done = bf16[4,160,512]{2,1,0:T(8,128)(2,1)S(1)} collective-permute-done((bf16[4,160,512]{2,1,0:T(8,128)(2,1)S(1)}, bf16[4,160,512]{2,1,0:T(8,128)(2,1)S(1)}, u32[]{:S(2)}, u32[]{:S(2)}) %collective-permute-start) | collective-permute-done | bytes 655392 | tf_op jit(solution)/shard_map/ppermute | solution.py:23
  60.1 9.8 %collective-permute-start.1 = (bf16[4,160,1024]{2,1,0:T(8,128)(2,1)S(1)}, bf16[4,160,1024]{2,1,0:T(8,128)(2,1)S(1)}, u32[]{:S(2)}, u32[]{:S(2)}) collective-permute-start(bf16[4,160,1024]{2,1,0:T(8,128)(2,1)S(1)} %pad_maximum_fusion.10), channel_id=1, source_target_pairs={{0,1},{1,0},{2,3},{3,2},{4,5},{5,4},{6,7},{7,6},{8,9},{9,8},{10,11... | collective-permute-start | bytes 3932168 | tf_op jit(solution)/shard_map/ppermute | solution.py:23
  70.4 31.6 %collective-permute-done.2 = bf16[4,160,512]{2,1,0:T(8,128)(2,1)S(1)} collective-permute-done((bf16[4,160,512]{2,1,0:T(8,128)(2,1)S(1)}, bf16[4,160,512]{2,1,0:T(8,128)(2,1)S(1)}, u32[]{:S(2)}, u32[]{:S(2)}) %collective-permute-start.2) | collective-permute-done | bytes 655392 | tf_op jit(solution)/shard_map/ppermute | solution.py:23
  102.2 9.8 %collective-permute-start.3 = (bf16[4,160,1024]{2,1,0:T(8,128)(2,1)S(1)}, bf16[4,160,1024]{2,1,0:T(8,128)(2,1)S(1)}, u32[]{:S(2)}, u32[]{:S(2)}) collective-permute-start(bf16[4,160,1024]{2,1,0:T(8,128)(2,1)S(1)} %pad_maximum_fusion.11), channel_id=1, source_target_pairs={{0,1},{1,0},{2,3},{3,2},{4,5},{5,4},{6,7},{7,6},{8,9},{9,8},{10,11... | collective-permute-start | bytes 3932168 | tf_op jit(solution)/shard_map/ppermute | solution.py:23
  113.2 1.4 collective-permute-start.14
  117.0 13.2 %collective-permute-done.4 = bf16[1280,512]{1,0:T(8,128)(2,1)S(1)} collective-permute-done((bf16[1280,512]{1,0:T(8,128)(2,1)S(1)}, bf16[1280,512]{1,0:T(8,128)(2,1)S(1)}, u32[]{:S(2)}, u32[]{:S(2)}) %collective-permute-start.4) | collective-permute-done | bytes 1310752 | tf_op jit(solution)/shard_map/ppermute | solution.py:23
  131.3 5.3 %collective-permute-start.12 = (bf16[2,320,640]{2,1,0:T(8,128)(2,1)S(1)}, bf16[2,320,640]{2,1,0:T(8,128)(2,1)S(1)}, u32[]{:S(2)}, u32[]{:S(2)}) collective-permute-start(bf16[2,320,640]{2,1,0:T(8,128)(2,1)S(1)} %convolution_convert_fusion.3), channel_id=1, source_target_pairs={{0,8},{2,10},{4,12},{6,14},{8,0},{10,2},{12,4},{14,6},{16,24},{18,... | collective-permute-start | bytes 2457608 | tf_op jit(solution)/shard_map/ppermute | solution.py:23
  138.2 1.7 collective-permute-start.5
  142.8 12.1 %collective-permute-done.5 = bf16[2,320,640]{2,1,0:T(8,128)(2,1)S(1)} collective-permute-done((bf16[2,320,640]{2,1,0:T(8,128)(2,1)S(1)}, bf16[2,320,640]{2,1,0:T(8,128)(2,1)S(1)}, u32[]{:S(2)}, u32[]{:S(2)}) %collective-permute-start.5) | collective-permute-done | bytes 819232 | tf_op jit(solution)/shard_map/ppermute | solution.py:23
  157.9 1.8 collective-permute-start.13
  160.8 8.8 %collective-permute-done.6 = bf16[320,640]{1,0:T(8,128)(2,1)S(1)} collective-permute-done((bf16[320,640]{1,0:T(8,128)(2,1)S(1)}, bf16[320,640]{1,0:T(8,128)(2,1)S(1)}, u32[]{:S(2)}, u32[]{:S(2)}) %collective-permute-start.6) | collective-permute-done | bytes 409632 | tf_op jit(solution)/shard_map/ppermute | solution.py:23
  172.5 2.3 multiply_convert_fusion.2
  174.8 1.8 collective-permute-start.16
  179.4 2.7 collective-permute-start.11
  184.0 1.4 dynamic-slice_reduce_fusion
  188.7 21.0 %collective-permute-done.30 = bf16[320,640]{1,0:T(8,128)(2,1)S(1)} collective-permute-done((bf16[320,640]{1,0:T(8,128)(2,1)S(1)}, bf16[320,640]{1,0:T(8,128)(2,1)S(1)}, u32[]{:S(2)}, u32[]{:S(2)}) %collective-permute-start.30) | collective-permute-done | bytes 409632 | tf_op jit(solution)/shard_map/ppermute | solution.py:23
  212.0 1.5 collective-permute-start.29
  213.5 1.5 pad_maximum_fusion.4
  215.5 2.0 fusion.80
  217.7 2.0 fusion.81
  221.9 1.5 collective-permute-start.20
  223.4 5.3 %collective-permute-done.29 = bf16[2,320,640]{2,1,0:T(8,128)(2,1)S(1)} collective-permute-done((bf16[2,320,640]{2,1,0:T(8,128)(2,1)S(1)}, bf16[2,320,640]{2,1,0:T(8,128)(2,1)S(1)}, u32[]{:S(2)}, u32[]{:S(2)}) %collective-permute-start.29) | collective-permute-done | bytes 819232 | tf_op jit(solution)/shard_map/ppermute | solution.py:23
  229.3 1.3 fusion.8
  230.8 1.6 copy-done.7
  232.3 1.9 fusion.82
  234.3 1.9 fusion.83
  236.2 1.4 fusion.3
  239.1 1.3 collective-permute-start.37
  241.6 1.5 collective-permute-start.34
  243.1 7.6 %all-reduce.1 = (f32[1024]{0:T(1024)S(1)}, f32[1024]{0:T(1024)S(1)}) all-reduce(f32[1024]{0:T(1024)S(1)} %maximum_add_fusion, f32[1024]{0:T(1024)S(1)} %maximum_add_fusion.1), channel_id=1, replica_groups=mesh['expert'=16,'ffn'=2] {'ffn'}, use_global_device_ids=true, to_apply=%region_3.4 | all-reduce | flops 2048 | bytes 16384 | tf_op jit(solution)/shard_map/psum | solution.py:153
  253.5 4.1 %add_reduce_fusion.3 = (f32[]{:T(128)}, f32[]{:T(128)}) fusion(f32[1024,640]{0,1:T(8,128)} %copy-done.5, f32[1024,640]{0,1:T(8,128)} %copy-done.4, f32[1280]{0:T(1024)S(1)} %broadcast_divide_fusion.1, f32[1024]{0:T(1024)S(1)} %get-tuple-element.27), kind=kLoop, calls=%fused_computation.19 | loop fusion | flops 9175038 | bytes 5252104 | tf_op jit(solution)/shard_map/reduce_sum | solution.py:185
  261.4 4.1 %add_reduce_fusion = (f32[]{:T(128)}, f32[]{:T(128)}) fusion(f32[640,1024]{1,0:T(8,128)S(1)} %copy-done.3, f32[640,1024]{1,0:T(8,128)S(1)} %fusion.82, f32[1024]{0:T(1024)S(1)} %get-tuple-element.25, f32[1280]{0:T(1024)S(1)} %broadcast_divide_fusion), kind=kLoop, calls=%fused_computation.16 | loop fusion | flops 9175038 | bytes 5252104 | tf_op jit(solution)/shard_map/reduce_sum | solution.py:171
  266.7 1.4 collective-permute-start.24
  269.5 2.0 collective-permute-start.40
  273.4 2.3 collective-permute-done.38
  275.6 1.3 add_add_fusion
  277.2 33.1 %collective-permute-done.27 = f32[2]{0:T(128)S(1)} collective-permute-done((f32[2]{0:T(128)S(1)}, f32[2]{0:T(128)S(1)}, u32[]{:S(2)}, u32[]{:S(2)}) %collective-permute-start.27) | collective-permute-done | bytes 40 | tf_op jit(solution)/shard_map/ppermute | solution.py:23
  311.5 4.5 %all-reduce = (f32[2]{0:T(128)S(1)}, f32[]{:T(128)}, f32[2]{0:T(128)S(1)}) all-reduce(f32[2]{0:T(128)S(1)} %add.218, f32[]{:T(128)} %dynamic-slice_reduce_fusion.1, f32[2]{0:T(128)S(1)} %add.231), channel_id=1, replica_groups=mesh['expert'=16,'ffn'=2] {'ffn'}, use_global_device_ids=true, to_apply=%region_8.9 | all-reduce | flops 5 | bytes 40 | tf_op jit(solution)/shard_map/psum | solution.py:47
  320.5 2.9 fusion.12
  323.4 1.9 maximum_select_fusion
  325.3 4.4 %copy.20 = bf16[1,512,2560]{2,1,0:T(8,128)(2,1)} copy(bf16[1,512,2560]{1,2,0:T(8,128)(2,1)} %maximum_select_fusion) | data formatting | bytes 5242880
  329.7 2.3 fusion.13
  332.0 1.9 maximum_select_fusion.1
  (166 shorter events, 55.3 us)
Async XLA Ops:
  4.8 21.8 %all-to-all-start.1 = ((bf16[16,40,512]{2,1,0:T(8,128)(2,1)}), bf16[16,40,512]{2,1,0:T(8,128)(2,1)S(1)}, u32[]{:S(2)}, u32[]{:S(2)}) async-start(bf16[16,40,512]{2,1,0:T(8,128)(2,1)} %bitcast.8), calls=%async_computation.1 | async-start | bytes 1310720 | tf_op jit(solution)/shard_map/all_to_all | solution.py:88
  26.6 20.3 %all-to-all-start = ((bf16[16,40,512]{2,1,0:T(8,128)(2,1)}), bf16[16,40,512]{2,1,0:T(8,128)(2,1)S(1)}, u32[]{:S(2)}, u32[]{:S(2)}) async-start(bf16[16,40,512]{2,1,0:T(8,128)(2,1)} %bitcast.2), calls=%async_computation | async-start | bytes 1310720 | tf_op jit(solution)/shard_map/all_to_all | solution.py:88
  47.3 12.6 %collective-permute-start = (bf16[4,160,512]{2,1,0:T(8,128)(2,1)S(1)}, bf16[4,160,512]{2,1,0:T(8,128)(2,1)S(1)}, u32[]{:S(2)}, u32[]{:S(2)}) collective-permute-start(bf16[4,160,512]{2,1,0:T(8,128)(2,1)S(1)} %bitcast.173), channel_id=1, source_target_pairs={{0,2},{2,0},{4,6},{6,4},{8,10},{10,8},{12,14},{14,12},{16,18},{18,... | collective-permute-start | bytes 1966088 | tf_op jit(solution)/shard_map/ppermute | solution.py:23
  50.2 61.8 %collective-permute-start.7 = (bf16[512,1280]{1,0:T(8,128)(2,1)S(1)}, bf16[512,1280]{1,0:T(8,128)(2,1)S(1)}, u32[]{:S(2)}, u32[]{:S(2)}) collective-permute-start(bf16[512,1280]{1,0:T(8,128)(2,1)S(1)} %get-tuple-element.30), channel_id=1, source_target_pairs={{0,2},{2,0},{4,6},{6,4},{8,10},{10,8},{12,14},{14,12},{16,18},{18,... | collective-permute-start | bytes 3932168 | tf_op jit(solution)/shard_map/ppermute | solution.py:23
  50.7 19.1 %copy-start.12 = (bf16[1,2560,512]{2,1,0:T(8,128)(2,1)S(1)}, bf16[1,2560,512]{2,1,0:T(8,128)(2,1)}, u32[]{:S(2)}) copy-start(bf16[1,2560,512]{2,1,0:T(8,128)(2,1)} %param.11) | copy-start | bytes 7864324
  50.9 51.1 %collective-permute-start.2 = (bf16[4,160,512]{2,1,0:T(8,128)(2,1)S(1)}, bf16[4,160,512]{2,1,0:T(8,128)(2,1)S(1)}, u32[]{:S(2)}, u32[]{:S(2)}) collective-permute-start(bf16[4,160,512]{2,1,0:T(8,128)(2,1)S(1)} %bitcast.168), channel_id=1, source_target_pairs={{0,2},{2,0},{4,6},{6,4},{8,10},{10,8},{12,14},{14,12},{16,18},{18,... | collective-permute-start | bytes 1966088 | tf_op jit(solution)/shard_map/ppermute | solution.py:23
  59.9 54.7 %copy-start.8 = (bf16[4,160,512]{2,1,0:T(8,128)(2,1)}, bf16[4,160,512]{2,1,0:T(8,128)(2,1)S(1)}, u32[]{:S(2)}) copy-start(bf16[4,160,512]{2,1,0:T(8,128)(2,1)S(1)} %collective-permute-done) | copy-start | bytes 1966084
  60.1 52.0 %collective-permute-start.1 = (bf16[4,160,1024]{2,1,0:T(8,128)(2,1)S(1)}, bf16[4,160,1024]{2,1,0:T(8,128)(2,1)S(1)}, u32[]{:S(2)}, u32[]{:S(2)}) collective-permute-start(bf16[4,160,1024]{2,1,0:T(8,128)(2,1)S(1)} %pad_maximum_fusion.10), channel_id=1, source_target_pairs={{0,1},{1,0},{2,3},{3,2},{4,5},{5,4},{6,7},{7,6},{8,9},{9,8},{10,11... | collective-permute-start | bytes 3932168 | tf_op jit(solution)/shard_map/ppermute | solution.py:23
  70.1 60.1 %collective-permute-start.4 = (bf16[1280,512]{1,0:T(8,128)(2,1)S(1)}, bf16[1280,512]{1,0:T(8,128)(2,1)S(1)}, u32[]{:S(2)}, u32[]{:S(2)}) collective-permute-start(bf16[1280,512]{1,0:T(8,128)(2,1)S(1)} %get-tuple-element.32), channel_id=1, source_target_pairs={{0,2},{2,0},{4,6},{6,4},{8,10},{10,8},{12,14},{14,12},{16,18},{18,... | collective-permute-start | bytes 3932168 | tf_op jit(solution)/shard_map/ppermute | solution.py:23
  102.2 27.9 %collective-permute-start.3 = (bf16[4,160,1024]{2,1,0:T(8,128)(2,1)S(1)}, bf16[4,160,1024]{2,1,0:T(8,128)(2,1)S(1)}, u32[]{:S(2)}, u32[]{:S(2)}) collective-permute-start(bf16[4,160,1024]{2,1,0:T(8,128)(2,1)S(1)} %pad_maximum_fusion.11), channel_id=1, source_target_pairs={{0,1},{1,0},{2,3},{3,2},{4,5},{5,4},{6,7},{7,6},{8,9},{9,8},{10,11... | collective-permute-start | bytes 3932168 | tf_op jit(solution)/shard_map/ppermute | solution.py:23
  113.2 26.7 %collective-permute-start.14 = (bf16[2,320,640]{2,1,0:T(8,128)(2,1)S(1)}, bf16[2,320,640]{2,1,0:T(8,128)(2,1)S(1)}, u32[]{:S(2)}, u32[]{:S(2)}) collective-permute-start(bf16[2,320,640]{2,1,0:T(8,128)(2,1)S(1)} %convolution_convert_fusion.2), channel_id=1, source_target_pairs={{0,8},{2,10},{4,12},{6,14},{8,0},{10,2},{12,4},{14,6},{16,24},{18,... | collective-permute-start | bytes 2457608 | tf_op jit(solution)/shard_map/ppermute | solution.py:23
  115.0 26.5 %copy-start.10 = (bf16[4,320,1024]{2,1,0:T(8,128)(2,1)}, bf16[4,320,1024]{2,1,0:T(8,128)(2,1)S(1)}, u32[]{:S(2)}) copy-start(bf16[4,320,1024]{2,1,0:T(8,128)(2,1)S(1)} %pad_maximum_fusion.2) | copy-start | bytes 7864324
  116.2 25.3 %collective-permute-start.8 = (bf16[2,320,640]{2,1,0:T(8,128)(2,1)S(1)}, bf16[2,320,640]{2,1,0:T(8,128)(2,1)S(1)}, u32[]{:S(2)}, u32[]{:S(2)}) collective-permute-start(bf16[2,320,640]{2,1,0:T(8,128)(2,1)S(1)} %convolution_convert_fusion.4), channel_id=1, source_target_pairs={{0,4},{2,6},{4,0},{6,2},{8,12},{10,14},{12,8},{14,10},{16,20},{18,... | collective-permute-start | bytes 2457608 | tf_op jit(solution)/shard_map/ppermute | solution.py:23
  131.3 25.2 %collective-permute-start.12 = (bf16[2,320,640]{2,1,0:T(8,128)(2,1)S(1)}, bf16[2,320,640]{2,1,0:T(8,128)(2,1)S(1)}, u32[]{:S(2)}, u32[]{:S(2)}) collective-permute-start(bf16[2,320,640]{2,1,0:T(8,128)(2,1)S(1)} %convolution_convert_fusion.3), channel_id=1, source_target_pairs={{0,8},{2,10},{4,12},{6,14},{8,0},{10,2},{12,4},{14,6},{16,24},{18,... | collective-permute-start | bytes 2457608 | tf_op jit(solution)/shard_map/ppermute | solution.py:23
  136.9 18.1 %copy-start.6 = (bf16[4,320,1024]{2,1,0:T(8,128)(2,1)}, bf16[4,320,1024]{2,1,0:T(8,128)(2,1)S(1)}, u32[]{:S(2)}) copy-start(bf16[4,320,1024]{2,1,0:T(8,128)(2,1)S(1)} %pad_maximum_fusion.3) | copy-start | bytes 7864324
  138.2 16.8 %collective-permute-start.5 = (bf16[2,320,640]{2,1,0:T(8,128)(2,1)S(1)}, bf16[2,320,640]{2,1,0:T(8,128)(2,1)S(1)}, u32[]{:S(2)}, u32[]{:S(2)}) collective-permute-start(bf16[2,320,640]{2,1,0:T(8,128)(2,1)S(1)} %convolution_convert_fusion.5), channel_id=1, source_target_pairs={{0,4},{2,6},{4,0},{6,2},{8,12},{10,14},{12,8},{14,10},{16,20},{18,... | collective-permute-start | bytes 2457608 | tf_op jit(solution)/shard_map/ppermute | solution.py:23
  141.2 30.4 %collective-permute-start.15 = (bf16[320,640]{1,0:T(8,128)(2,1)S(1)}, bf16[320,640]{1,0:T(8,128)(2,1)S(1)}, u32[]{:S(2)}, u32[]{:S(2)}) collective-permute-start(bf16[320,640]{1,0:T(8,128)(2,1)S(1)} %fusion.45), channel_id=1, source_target_pairs={{0,4},{2,6},{4,0},{6,2},{8,12},{10,14},{12,8},{14,10},{16,20},{18,... | collective-permute-start | bytes 1228808 | tf_op jit(solution)/shard_map/ppermute | solution.py:23
  142.7 18.1 %collective-permute-start.9 = (bf16[320,640]{1,0:T(8,128)(2,1)S(1)}, bf16[320,640]{1,0:T(8,128)(2,1)S(1)}, u32[]{:S(2)}, u32[]{:S(2)}) collective-permute-start(bf16[320,640]{1,0:T(8,128)(2,1)S(1)} %fusion.43), channel_id=1, source_target_pairs={{0,8},{2,10},{4,12},{6,14},{8,0},{10,2},{12,4},{14,6},{16,24},{18,... | collective-permute-start | bytes 1228808 | tf_op jit(solution)/shard_map/ppermute | solution.py:23
  156.3 13.3 %collective-permute-start.6 = (bf16[320,640]{1,0:T(8,128)(2,1)S(1)}, bf16[320,640]{1,0:T(8,128)(2,1)S(1)}, u32[]{:S(2)}, u32[]{:S(2)}) collective-permute-start(bf16[320,640]{1,0:T(8,128)(2,1)S(1)} %fusion.42), channel_id=1, source_target_pairs={{0,8},{2,10},{4,12},{6,14},{8,0},{10,2},{12,4},{14,6},{16,24},{18,... | collective-permute-start | bytes 1228808 | tf_op jit(solution)/shard_map/ppermute | solution.py:23
  157.9 14.6 %collective-permute-start.13 = (bf16[320,640]{1,0:T(8,128)(2,1)S(1)}, bf16[320,640]{1,0:T(8,128)(2,1)S(1)}, u32[]{:S(2)}, u32[]{:S(2)}) collective-permute-start(bf16[320,640]{1,0:T(8,128)(2,1)S(1)} %fusion.44), channel_id=1, source_target_pairs={{0,4},{2,6},{4,0},{6,2},{8,12},{10,14},{12,8},{14,10},{16,20},{18,... | collective-permute-start | bytes 1228808 | tf_op jit(solution)/shard_map/ppermute | solution.py:23
  170.3 7.2 %collective-permute-start.10 = (bf16[320,640]{1,0:T(8,128)(2,1)S(1)}, bf16[320,640]{1,0:T(8,128)(2,1)S(1)}, u32[]{:S(2)}, u32[]{:S(2)}) collective-permute-start(bf16[320,640]{1,0:T(8,128)(2,1)S(1)} %get-tuple-element.34), channel_id=1, source_target_pairs={{0,8},{2,10},{4,12},{6,14},{8,0},{10,2},{12,4},{14,6},{16,24},{18,... | collective-permute-start | bytes 1228808 | tf_op jit(solution)/shard_map/ppermute | solution.py:23
  174.8 12.1 %collective-permute-start.16 = (bf16[320,640]{1,0:T(8,128)(2,1)S(1)}, bf16[320,640]{1,0:T(8,128)(2,1)}, u32[]{:S(2)}, u32[]{:S(2)}) collective-permute-start(bf16[320,640]{1,0:T(8,128)(2,1)S(1)} %get-tuple-element.36), channel_id=1, source_target_pairs={{0,4},{2,6},{4,0},{6,2},{8,12},{10,14},{12,8},{14,10},{16,20},{18,... | collective-permute-start | bytes 1228808 | tf_op jit(solution)/shard_map/ppermute | solution.py:23
  179.4 34.1 %collective-permute-start.11 = (bf16[2,320,640]{2,1,0:T(8,128)(2,1)S(1)}, bf16[2,320,640]{2,1,0:T(8,128)(2,1)}, u32[]{:S(2)}, u32[]{:S(2)}) collective-permute-start(bf16[2,320,640]{2,1,0:T(8,128)(2,1)S(1)} %get-tuple-element.42), channel_id=1, source_target_pairs={{0,4},{2,6},{4,0},{6,2},{8,12},{10,14},{12,8},{14,10},{16,20},{18,... | collective-permute-start | bytes 2457608 | tf_op jit(solution)/shard_map/ppermute | solution.py:23
  183.0 26.7 %collective-permute-start.30 = (bf16[320,640]{1,0:T(8,128)(2,1)S(1)}, bf16[320,640]{1,0:T(8,128)(2,1)S(1)}, u32[]{:S(2)}, u32[]{:S(2)}) collective-permute-start(bf16[320,640]{1,0:T(8,128)(2,1)S(1)} %get-tuple-element.35), channel_id=1, source_target_pairs={{0,4},{2,6},{4,0},{6,2},{8,12},{10,14},{12,8},{14,10},{16,20},{18,... | collective-permute-start | bytes 1228808 | tf_op jit(solution)/shard_map/ppermute | solution.py:23
  183.1 27.8 %collective-permute-start.28 = (bf16[320,640]{1,0:T(8,128)(2,1)S(1)}, bf16[320,640]{1,0:T(8,128)(2,1)}, u32[]{:S(2)}, u32[]{:S(2)}) collective-permute-start(bf16[320,640]{1,0:T(8,128)(2,1)S(1)} %get-tuple-element.33), channel_id=1, source_target_pairs={{0,8},{2,10},{4,12},{6,14},{8,0},{10,2},{12,4},{14,6},{16,24},{18,... | collective-permute-start | bytes 1228808 | tf_op jit(solution)/shard_map/ppermute | solution.py:23
  188.1 29.5 %collective-permute-start.17 = (bf16[2,320,640]{2,1,0:T(8,128)(2,1)S(1)}, bf16[2,320,640]{2,1,0:T(8,128)(2,1)S(1)}, u32[]{:S(2)}, u32[]{:S(2)}) collective-permute-start(bf16[2,320,640]{2,1,0:T(8,128)(2,1)S(1)} %get-tuple-element.44), channel_id=1, source_target_pairs={{0,8},{2,10},{4,12},{6,14},{8,0},{10,2},{12,4},{14,6},{16,24},{18,... | collective-permute-start | bytes 2457608 | tf_op jit(solution)/shard_map/ppermute | solution.py:23
  209.9 20.7 %collective-permute-start.31 = (bf16[2,320,640]{2,1,0:T(8,128)(2,1)S(1)}, bf16[2,320,640]{2,1,0:T(8,128)(2,1)S(1)}, u32[]{:S(2)}, u32[]{:S(2)}) collective-permute-start(bf16[2,320,640]{2,1,0:T(8,128)(2,1)S(1)} %get-tuple-element.40), channel_id=1, source_target_pairs={{0,8},{2,10},{4,12},{6,14},{8,0},{10,2},{12,4},{14,6},{16,24},{18,... | collective-permute-start | bytes 2457608 | tf_op jit(solution)/shard_map/ppermute | solution.py:23
  212.0 16.6 %collective-permute-start.29 = (bf16[2,320,640]{2,1,0:T(8,128)(2,1)S(1)}, bf16[2,320,640]{2,1,0:T(8,128)(2,1)S(1)}, u32[]{:S(2)}, u32[]{:S(2)}) collective-permute-start(bf16[2,320,640]{2,1,0:T(8,128)(2,1)S(1)} %get-tuple-element.38), channel_id=1, source_target_pairs={{0,4},{2,6},{4,0},{6,2},{8,12},{10,14},{12,8},{14,10},{16,20},{18,... | collective-permute-start | bytes 2457608 | tf_op jit(solution)/shard_map/ppermute | solution.py:23
  220.7 30.1 %collective-permute-start.22 = (f32[1280]{0:T(1024)S(1)}, f32[1280]{0:T(1024)S(1)}, u32[]{:S(2)}, u32[]{:S(2)}) collective-permute-start(f32[1280]{0:T(1024)S(1)} %get-tuple-element.13), channel_id=1, source_target_pairs={{0,12},{2,14},{4,8},{6,10},{8,4},{10,6},{12,0},{14,2},{16,28},{18,... | collective-permute-start | bytes 15368 | tf_op jit(solution)/shard_map/ppermute | solution.py:23
  221.0 31.0 %collective-permute-start.21 = (f32[1280]{0:T(1024)S(1)}, f32[1280]{0:T(1024)S(1)}, u32[]{:S(2)}, u32[]{:S(2)}) collective-permute-start(f32[1280]{0:T(1024)S(1)} %get-tuple-element.13), channel_id=1, source_target_pairs={{0,8},{2,10},{4,12},{6,14},{8,0},{10,2},{12,4},{14,6},{16,24},{18,... | collective-permute-start | bytes 15368 | tf_op jit(solution)/shard_map/ppermute | solution.py:23
  221.9 31.2 %collective-permute-start.20 = (f32[1280]{0:T(1024)S(1)}, f32[1280]{0:T(1024)S(1)}, u32[]{:S(2)}, u32[]{:S(2)}) collective-permute-start(f32[1280]{0:T(1024)S(1)} %get-tuple-element.13), channel_id=1, source_target_pairs={{0,4},{2,6},{4,0},{6,2},{8,12},{10,14},{12,8},{14,10},{16,20},{18,... | collective-permute-start | bytes 15368 | tf_op jit(solution)/shard_map/ppermute | solution.py:23
  229.0 11.4 %collective-permute-start.19 = (f32[1024]{0:T(1024)S(1)}, f32[1024]{0:T(1024)S(1)}, u32[]{:S(2)}, u32[]{:S(2)}) collective-permute-start(f32[1024]{0:T(1024)S(1)} %get-tuple-element.12), channel_id=1, source_target_pairs={{0,2},{2,0},{4,6},{6,4},{8,10},{10,8},{12,14},{14,12},{16,18},{18,... | collective-permute-start | bytes 12296 | tf_op jit(solution)/shard_map/ppermute | solution.py:23
  239.1 2.5 collective-permute-start.37
  240.4 18.5 %collective-permute-start.35 = (f32[1280]{0:T(1024)S(1)}, f32[1280]{0:T(1024)S(1)}, u32[]{:S(2)}, u32[]{:S(2)}) collective-permute-start(f32[1280]{0:T(1024)S(1)} %get-tuple-element.8), channel_id=1, source_target_pairs={{0,12},{2,14},{4,8},{6,10},{8,4},{10,6},{12,0},{14,2},{16,28},{18,... | collective-permute-start | bytes 15368 | tf_op jit(solution)/shard_map/ppermute | solution.py:23
  241.6 18.4 %collective-permute-start.34 = (f32[1280]{0:T(1024)S(1)}, f32[1280]{0:T(1024)S(1)}, u32[]{:S(2)}, u32[]{:S(2)}) collective-permute-start(f32[1280]{0:T(1024)S(1)} %get-tuple-element.8), channel_id=1, source_target_pairs={{0,8},{2,10},{4,12},{6,14},{8,0},{10,2},{12,4},{14,6},{16,24},{18,... | collective-permute-start | bytes 15368 | tf_op jit(solution)/shard_map/ppermute | solution.py:23
  250.8 10.2 %collective-permute-start.33 = (f32[1280]{0:T(1024)S(1)}, f32[1280]{0:T(1024)S(1)}, u32[]{:S(2)}, u32[]{:S(2)}) collective-permute-start(f32[1280]{0:T(1024)S(1)} %get-tuple-element.8), channel_id=1, source_target_pairs={{0,4},{2,6},{4,0},{6,2},{8,12},{10,14},{12,8},{14,10},{16,20},{18,... | collective-permute-start | bytes 15368 | tf_op jit(solution)/shard_map/ppermute | solution.py:23
  252.0 68.5 %collective-permute-start.18 = (bf16[512,1280]{0,1:T(8,128)(2,1)}, bf16[512,1280]{0,1:T(8,128)(2,1)}, u32[]{:S(2)}, u32[]{:S(2)}) collective-permute-start(bf16[512,1280]{0,1:T(8,128)(2,1)} %fusion.8), channel_id=1, source_target_pairs={{0,2},{2,0},{4,6},{6,4},{8,10},{10,8},{12,14},{14,12},{16,18},{18,... | collective-permute-start | bytes 3932168 | tf_op jit(solution)/shard_map/ppermute | solution.py:23
  253.2 76.5 %collective-permute-start.32 = (bf16[1280,512]{1,0:T(8,128)(2,1)}, bf16[1280,512]{1,0:T(8,128)(2,1)}, u32[]{:S(2)}, u32[]{:S(2)}) collective-permute-start(bf16[1280,512]{1,0:T(8,128)(2,1)} %fusion.3), channel_id=1, source_target_pairs={{0,2},{2,0},{4,6},{6,4},{8,10},{10,8},{12,14},{14,12},{16,18},{18,... | collective-permute-start | bytes 3932168 | tf_op jit(solution)/shard_map/ppermute | solution.py:23
  258.9 61.6 %collective-permute-start.23 = (f32[1280]{0:T(1024)S(1)}, f32[1280]{0:T(1024)S(1)}, u32[]{:S(2)}, u32[]{:S(2)}) collective-permute-start(f32[1280]{0:T(1024)S(1)} %get-tuple-element.24), channel_id=1, source_target_pairs={{0,2},{2,0},{4,6},{6,4},{8,10},{10,8},{12,14},{14,12},{16,18},{18,... | collective-permute-start | bytes 15368 | tf_op jit(solution)/shard_map/ppermute | solution.py:23
  260.1 6.7 %collective-permute-start.25 = (f32[2]{0:T(128)S(1)}, f32[2]{0:T(128)S(1)}, u32[]{:S(2)}, u32[]{:S(2)}) collective-permute-start(f32[2]{0:T(128)S(1)} %pad_maximum_fusion.17), channel_id=1, source_target_pairs={{0,8},{2,10},{4,12},{6,14},{8,0},{10,2},{12,4},{14,6},{16,24},{18,... | collective-permute-start | bytes 32 | tf_op jit(solution)/shard_map/ppermute | solution.py:23
  261.0 7.1 %collective-permute-start.26 = (f32[2]{0:T(128)S(1)}, f32[2]{0:T(128)S(1)}, u32[]{:S(2)}, u32[]{:S(2)}) collective-permute-start(f32[2]{0:T(128)S(1)} %pad_maximum_fusion.17), channel_id=1, source_target_pairs={{0,12},{2,14},{4,8},{6,10},{8,4},{10,6},{12,0},{14,2},{16,28},{18,... | collective-permute-start | bytes 32 | tf_op jit(solution)/shard_map/ppermute | solution.py:23
  266.7 2.8 collective-permute-start.24
  268.1 4.7 %collective-permute-start.39 = (f32[2]{0:T(128)S(1)}, f32[2]{0:T(128)S(1)}, u32[]{:S(2)}, u32[]{:S(2)}) collective-permute-start(f32[2]{0:T(128)S(1)} %pad_maximum_fusion.18), channel_id=1, source_target_pairs={{0,8},{2,10},{4,12},{6,14},{8,0},{10,2},{12,4},{14,6},{16,24},{18,... | collective-permute-start | bytes 32 | tf_op jit(solution)/shard_map/ppermute | solution.py:23
  269.5 3.4 %collective-permute-start.40 = (f32[2]{0:T(128)S(1)}, f32[2]{0:T(128)S(1)}, u32[]{:S(2)}, u32[]{:S(2)}) collective-permute-start(f32[2]{0:T(128)S(1)} %pad_maximum_fusion.18), channel_id=1, source_target_pairs={{0,12},{2,14},{4,8},{6,10},{8,4},{10,6},{12,0},{14,2},{16,28},{18,... | collective-permute-start | bytes 32 | tf_op jit(solution)/shard_map/ppermute | solution.py:23
  272.8 2.8 collective-permute-start.38
  272.9 37.3 %collective-permute-start.27 = (f32[2]{0:T(128)S(1)}, f32[2]{0:T(128)S(1)}, u32[]{:S(2)}, u32[]{:S(2)}) collective-permute-start(f32[2]{0:T(128)S(1)} %add_add_fusion.1), channel_id=1, source_target_pairs={{0,2},{2,0},{4,6},{6,4},{8,10},{10,8},{12,14},{14,12},{16,18},{18,... | collective-permute-start | bytes 32 | tf_op jit(solution)/shard_map/ppermute | solution.py:23
  276.9 33.3 %collective-permute-start.41 = (f32[2]{0:T(128)S(1)}, f32[2]{0:T(128)S(1)}, u32[]{:S(2)}, u32[]{:S(2)}) collective-permute-start(f32[2]{0:T(128)S(1)} %add_add_fusion), channel_id=1, source_target_pairs={{0,2},{2,0},{4,6},{6,4},{8,10},{10,8},{12,14},{14,12},{16,18},{18,... | collective-permute-start | bytes 32 | tf_op jit(solution)/shard_map/ppermute | solution.py:23
  310.3 10.2 %collective-permute-start.36 = (f32[1280]{0:T(1024)S(1)}, f32[1280]{0:T(1024)S(1)}, u32[]{:S(2)}, u32[]{:S(2)}) collective-permute-start(f32[1280]{0:T(1024)S(1)} %get-tuple-element.22), channel_id=1, source_target_pairs={{0,2},{2,0},{4,6},{6,4},{8,10},{10,8},{12,14},{14,12},{16,18},{18,... | collective-permute-start | bytes 15368 | tf_op jit(solution)/shard_map/ppermute | solution.py:23
  (14 other events, 82.1 us)
